TPU v7x, 32 devices: a whole 2x2x4 slice. The times are simulated.
32 devices in a mesh: row: 8 (over z, y), col: 4 (over x, core).
Axes of the slice: x: 2, y: 2, z: 4, core: 2. Of those that a mesh axis runs over, the one named last changes fastest.
Arguments:
- factor: float32 [1024, 1024], P('row', 'col'), may hold values from -0.375 to 0.375
- rhs: float32 [1024, 512], P('row', 'col'), may hold values from -6 to 6
- parent: int32 [7], replicated, may hold values from 4 to 6, as said below
- bounds: int32 [8], replicated, may hold values from 0 to 8, as said below
- slot: int32 [8], replicated, may hold values from 0 to 7, each once
- structure: int32 [7, 8], replicated, may hold values 0 or 1
Outputs:
- solution: float32 [1024, 512], P('row', 'col')
Inputs may be any that keep to these rules, and one draw needn't show every extreme that they name: parent[s] is 4 or 5 for s = 0 to 3, and 6 for s = 4, 5, 6 (the root is its own entry). bounds[0] = 0, bounds[7] = 8, strictly increasing; supernode s holds logical blocks bounds[s] to bounds[s+1] - 1. `slot`: a permutation.
All inputs are finite; a program needn't handle non-finite values.
Results may differ from a plain program's by a relative error of at most 0.0001.
Values sent between devices are 32-bit elements; how exact they have to be, the bound alone decides.
No kernel may reach another device: no remote copies, remote signals or barrier semaphores. Data moves between devices by JAX's collectives and lax.ppermute only.
A program may use at most 64 MiB of HBM per device.

v0:
```python
import jax
import jax.numpy as jnp
from jax import lax
from jax.sharding import PartitionSpec as P

B = 128
RB = 1


def block_masks(parent, bounds, slot, structure):
    count = slot.shape[0]
    ar = jnp.arange(count, dtype=jnp.int32)
    logical = jnp.sum(jnp.where(slot[:, None] == ar[None, :], ar[:, None], 0), axis=0)
    node = jnp.sum((logical[:, None] >= bounds[None, 1:7]).astype(jnp.int32), axis=1)
    level = (node >= 4).astype(jnp.int32) + (node >= 6).astype(jnp.int32)
    nodes = jnp.arange(7, dtype=jnp.int32)
    grand = parent[parent]
    ancestor = ((nodes[None, :] == parent[:, None]) | (nodes[None, :] == grand[:, None])) & (
        nodes[None, :] != nodes[:, None]
    )
    node_hot = (node[:, None] == nodes[None, :]).astype(jnp.float32)
    perm_hot = (logical[:, None] == ar[None, :]).astype(jnp.float32)
    listed_store = jnp.dot(
        structure.astype(jnp.float32), perm_hot.T, precision=lax.Precision.HIGHEST
    )
    anc_pairs = jnp.dot(
        node_hot,
        jnp.dot(ancestor.astype(jnp.float32), node_hot.T, precision=lax.Precision.HIGHEST),
        precision=lax.Precision.HIGHEST,
    )
    list_pairs = jnp.dot(node_hot, listed_store, precision=lax.Precision.HIGHEST)
    link = (anc_pairs * list_pairs).T > 0.5
    same = node[:, None] == node[None, :]
    return (level, same, link)


def masked(block_rows, mask):
    rblocks, width = mask.shape
    bsz = block_rows.shape[0] // rblocks
    shaped = block_rows.reshape(rblocks, bsz, width, bsz) * mask[:, None, :, None].astype(
        jnp.float32
    )
    return shaped.reshape(block_rows.shape)


def body(factor, rhs, parent, bounds, slot, structure):
    level, same, link = block_masks(parent, bounds, slot, structure)
    first = lax.axis_index("row") * RB
    level_mine = lax.dynamic_slice_in_dim(level, first, RB, 0)
    same_mine = lax.dynamic_slice_in_dim(same, first, RB, 0)
    link_mine = lax.dynamic_slice_in_dim(link, first, RB, 0)
    full_rows = lax.all_gather(factor, "col", axis=1, tiled=True)
    diag_part = masked(full_rows, same_mine)
    link_part = masked(full_rows, link_mine)

    def product(matrix, vector):
        return jnp.dot(
            matrix,
            lax.all_gather(vector, "row", axis=0, tiled=True),
            precision=lax.Precision.HIGHEST,
            preferred_element_type=jnp.float32,
        )

    pieces = [rhs]
    accums = [jnp.zeros(p.shape, jnp.float32) for p in pieces]
    results = [jnp.zeros(p.shape, jnp.float32) for p in pieces]
    for section in range(3):
        rows = jnp.repeat(level_mine == section, B)[:, None]
        solved = jnp.where(rows, product(diag_part, pieces[0] - accums[0]), 0.0)
        results[0] = results[0] + solved
        if section < 2:
            accums[0] = accums[0] + product(link_part, solved)
    return results[0]


def solution(mesh):
    in_specs = (P("row", "col"), P("row", "col"), P(), P(), P(), P())
    out_specs = P("row", "col")
    return jax.shard_map(body, mesh=mesh, in_specs=in_specs, out_specs=out_specs, check_vma=False)
```

profile of v0, /device:TPU:0, one launch (start us, length us, event | category | flops | bytes accessed | tf_op | source)
XLA Modules:
  0.0 176.7 jit_solution(1888394045986207632)
XLA Ops:
  0.0 0.0 copy-start.4
  0.0 0.7 copy-done.4
  0.7 0.0 copy-start.5
  0.7 0.1 select_reduce_fusion
  0.7 0.6 copy-done.5
  1.3 0.1 slice.3
  1.4 0.2 convert_reduce_fusion
  1.6 0.6 dynamic_slice.9
  4.1 0.0 copy-start
  4.1 0.6 copy-done
  4.8 0.1 broadcast_compare_fusion
  4.9 0.1 broadcast_bitcast_fusion.1
  4.9 0.6 gather_fusion
  5.6 0.2 fusion.17
  5.8 0.2 fusion.16
  6.0 0.3 copy-done.3
  6.3 0.2 fusion.14
  6.5 0.2 fusion.2
  6.7 0.1 broadcast_bitcast_fusion
  6.7 0.0 copy-done.2
  6.7 8.7 %all_gather.18 = f32[128,1024]{1,0:T(8,128)S(1)} all-gather(f32[128,256]{1,0:T(8,128)S(1)} %copy-done.2), channel_id=1, replica_groups=mesh['row'=8,'col'=4] {'col'}, dimensions={1}, use_global_device_ids=true | all-gather | bytes 655360 | tf_op jit(solution)/shard_map/all_gather | solution.py:52
  15.5 0.0 copy-done.1
  15.5 31.9 %all_gather.19 = f32[1024,128]{1,0:T(8,128)S(1)} all-gather(f32[128,128]{1,0:T(8,128)S(1)} %copy-done.1), channel_id=1, replica_groups=mesh['row'=8,'col'=4] {'row'}, dimensions={0}, use_global_device_ids=true | all-gather | bytes 589824 | tf_op jit(solution)/shard_map/all_gather | solution.py:59
  47.4 0.7 convolution_select_fusion.2
  48.0 31.5 %all_gather.20 = f32[1024,128]{1,0:T(8,128)S(1)} all-gather(f32[128,128]{1,0:T(8,128)S(1)} %convolution_select_fusion.2), channel_id=1, replica_groups=mesh['row'=8,'col'=4] {'row'}, dimensions={0}, use_global_device_ids=true | all-gather | bytes 589824 | tf_op jit(solution)/shard_map/all_gather | solution.py:59
  79.5 0.7 fusion.30
  80.2 31.3 %all_gather.21 = f32[1024,128]{1,0:T(8,128)S(1)} all-gather(f32[128,128]{1,0:T(8,128)S(1)} %get-tuple-element.5), channel_id=1, replica_groups=mesh['row'=8,'col'=4] {'row'}, dimensions={0}, use_global_device_ids=true | all-gather | bytes 589824 | tf_op jit(solution)/shard_map/all_gather | solution.py:59
  111.4 0.7 convolution_select_fusion.1
  112.1 31.5 %all_gather.22 = f32[1024,128]{1,0:T(8,128)S(1)} all-gather(f32[128,128]{1,0:T(8,128)S(1)} %convolution_select_fusion.1), channel_id=1, replica_groups=mesh['row'=8,'col'=4] {'row'}, dimensions={0}, use_global_device_ids=true | all-gather | bytes 589824 | tf_op jit(solution)/shard_map/all_gather | solution.py:59
  143.6 0.7 fusion.1
  144.3 31.2 %all_gather.23 = f32[1024,128]{1,0:T(8,128)S(1)} all-gather(f32[128,128]{1,0:T(8,128)S(1)} %fusion.1), channel_id=1, replica_groups=mesh['row'=8,'col'=4] {'row'}, dimensions={0}, use_global_device_ids=true | all-gather | bytes 589824 | tf_op jit(solution)/shard_map/all_gather | solution.py:59
  175.4 1.3 fusion
  (8 shorter events, 0.0 us)
Async XLA Ops:
  0.0 0.7 copy-start.4
  0.7 0.7 copy-start.5
  4.1 0.7 copy-start
  5.6 0.7 copy-start.3
  5.8 1.0 copy-start.2
  6.7 8.7 %copy-start.1 = (f32[128,128]{1,0:T(8,128)S(1)}, f32[128,128]{1,0:T(8,128)}, u32[]{:S(2)}) copy-start(f32[128,128]{1,0:T(8,128)} %param.7) | copy-start | bytes 196612
where the time goes:
time: 177 us
  blocking collectives  166 us (94%)
  matrix products  4.68 us (3%)
  local copies, waits for them, and re-layouts  3.63 us (2%)
  between operations  2 us (1%)
    all_gather x5, blocking collectives, product(): lax.all_gather(vector, 'row', axis=0, tiled=True)  157 us
    all_gather x1, blocking collectives, body(): full_rows = lax.all_gather(factor, 'col', axis=1, tiled=True)  8.74 us
    dot_general x5, matrix products, product(): jnp.dot(matrix, lax.all_gather(vector, 'row', axis=0, tiled=True), precis...  3.93 us

commit v1 on v0

v1 whole, which is shorter than its diff:
```python
import functools

import jax
import jax.numpy as jnp
from jax import lax
from jax.experimental import pallas as pl
from jax.experimental.pallas import tpu as pltpu
from jax.sharding import PartitionSpec as P

SMEM = pl.BlockSpec(memory_space=pltpu.SMEM)
VMEM = pl.BlockSpec(memory_space=pltpu.VMEM)
HIGHEST = lax.Precision.HIGHEST


def block_masks(parent, bounds, slot, structure):
    count = slot.shape[0]
    ar = jnp.arange(count, dtype=jnp.int32)
    logical = jnp.sum(jnp.where(slot[:, None] == ar[None, :], ar[:, None], 0), axis=0)
    node = jnp.sum((logical[:, None] >= bounds[None, 1:7]).astype(jnp.int32), axis=1)
    level = (node >= 4).astype(jnp.int32) + (node >= 6).astype(jnp.int32)
    nodes = jnp.arange(7, dtype=jnp.int32)
    grand = parent[parent]
    ancestor = ((nodes[None, :] == parent[:, None]) | (nodes[None, :] == grand[:, None])) & (
        nodes[None, :] != nodes[:, None]
    )
    node_hot = (node[:, None] == nodes[None, :]).astype(jnp.float32)
    perm_hot = (logical[:, None] == ar[None, :]).astype(jnp.float32)
    listed_store = jnp.dot(structure.astype(jnp.float32), perm_hot.T, precision=HIGHEST)
    anc_pairs = jnp.dot(
        node_hot, jnp.dot(ancestor.astype(jnp.float32), node_hot.T, precision=HIGHEST), precision=HIGHEST
    )
    list_pairs = jnp.dot(node_hot, listed_store, precision=HIGHEST)
    link = (anc_pairs * list_pairs).T > 0.5
    same = node[:, None] == node[None, :]
    return level, same, link


def masked(block_rows, mask):
    rblocks, width = mask.shape
    bsz = block_rows.shape[0] // rblocks
    shaped = block_rows.reshape(rblocks, bsz, width, bsz) * mask[:, None, :, None].astype(jnp.float32)
    return shaped.reshape(block_rows.shape)


def general_body(factor, rhs, parent, bounds, slot, structure, n_row):
    level, same, link = block_masks(parent, bounds, slot, structure)
    held = slot.shape[0] // n_row
    bsz = factor.shape[0] // held
    first = lax.axis_index("row") * held
    level_mine = lax.dynamic_slice_in_dim(level, first, held, 0)
    same_mine = lax.dynamic_slice_in_dim(same, first, held, 0)
    link_mine = lax.dynamic_slice_in_dim(link, first, held, 0)
    full_rows = lax.all_gather(factor, "col", axis=1, tiled=True)
    diag_part = masked(full_rows, same_mine)
    link_part = masked(full_rows, link_mine)

    def product(matrix, vector):
        return jnp.dot(
            matrix,
            lax.all_gather(vector, "row", axis=0, tiled=True),
            precision=HIGHEST,
            preferred_element_type=jnp.float32,
        )

    acc = jnp.zeros(rhs.shape, jnp.float32)
    result = jnp.zeros(rhs.shape, jnp.float32)
    for section in range(3):
        rows = jnp.repeat(level_mine == section, bsz)[:, None]
        solved = jnp.where(rows, product(diag_part, rhs - acc), 0.0)
        result = result + solved
        if section < 2:
            acc = acc + product(link_part, solved)
    return result


MASK = 0
SAME = 1
LEVEL = 2
LINK = 4
FACTS = 32


def facts_kernel(parent, bounds, slot, structure, factor, rhs, facts, packed, logical):
    width = factor.shape[1]
    packed[:, :width] = factor[...]
    packed[:, width:] = rhs[...]
    p = lax.axis_index("row")
    c = lax.axis_index("col")
    for i in range(8):
        logical[slot[i]] = i
    wide = jnp.int32(0)
    for s in range(1, 7):
        wide = wide + (bounds[s] == s).astype(jnp.int32)
    m = slot[wide] ^ slot[wide + 1]
    facts[MASK] = m

    def node_of(q):
        at = logical[q]
        total = jnp.int32(0)
        for s in range(1, 7):
            total = total + (at >= bounds[s]).astype(jnp.int32)
        return total

    nodes = [node_of(p), node_of(p ^ m)]
    places = [logical[p], logical[p ^ m]]
    facts[SAME] = (nodes[0] == nodes[1]).astype(jnp.int32)
    for r in range(2):
        facts[LEVEL + r] = (nodes[r] >= 4).astype(jnp.int32) + (nodes[r] >= 6).astype(jnp.int32)
    for k in range(8):
        below = node_of(k ^ (2 * c))
        up = parent[below]
        top = parent[up]
        for r in range(2):
            above = ((nodes[r] == up) | (nodes[r] == top)) & (nodes[r] != below)
            listed = structure[below, places[r]] == 1
            facts[LINK + 8 * r + k] = (above & listed).astype(jnp.int32)


def take_diagonal(p, c, m, rows, diag, bsz):
    for r in range(2):
        for s in range(2):
            place = (p ^ (2 * c)) if s == 0 else (p ^ m ^ (2 * c))
            for k in range(8):

                @pl.when(place == k)
                def _(r=r, s=s, k=k):
                    at = (k % 2) * bsz
                    diag[r, s] = rows[r][k // 2][:, at : at + bsz]


def dot(a, b):
    return jnp.dot(a, b, precision=HIGHEST, preferred_element_type=jnp.float32)


def solve_pair(facts, diag, section, mine, pair):
    same = facts[SAME].astype(jnp.float32)
    on = [(facts[LEVEL + r] == section).astype(jnp.float32) for r in range(2)]
    y_mine = (dot(diag[0, 0], mine) + same * dot(diag[0, 1], pair)) * on[0]
    y_pair = (dot(diag[1, 1], pair) + same * dot(diag[1, 0], mine)) * on[1]
    return y_mine, y_pair


def first_kernel(facts, rhs, f0, f1, f2, f3, g0, g1, g2, g3, y, diag):
    bsz = rhs.shape[0]
    p = lax.axis_index("row")
    c = lax.axis_index("col")
    take_diagonal(p, c, facts[MASK], [[f0, f1, f2, f3], [g0, g1, g2, g3]], diag, bsz)
    y_mine, y_pair = solve_pair(facts, diag, 0, rhs[...], g0[:, 2 * bsz :])
    y[:bsz] = y_mine
    y[bsz:] = y_pair


def update(facts, rows, ys, picks, y_all, link, bsz):
    p = lax.axis_index("row")
    c = lax.axis_index("col")
    m = facts[MASK]
    for y, pick in zip(ys, picks):
        for s in range(2):
            place = p ^ pick ^ (2 * c) ^ (m if s else 0)
            y_all[pl.ds(pl.multiple_of(place * bsz, bsz), bsz), :] = y[s * bsz : (s + 1) * bsz, :]
    for r in range(2):
        for k in range(8):
            at = (k % 2) * bsz
            on = facts[LINK + 8 * r + k].astype(jnp.float32)
            link[r * bsz : (r + 1) * bsz, k * bsz : (k + 1) * bsz] = rows[r][k // 2][:, at : at + bsz] * on
    return dot(link[...], y_all[...])


def coset_picks(m):
    first = jnp.where(m == 1, 2, 1)
    second = jnp.where(m >= 4, 2, 4)
    return [0, first, second, first ^ second]


def second_kernel(facts, rhs, f0, f1, f2, f3, g0, g1, g2, g3, y, ya, yb, yc, y1, t, diag, y_all, link):
    bsz = rhs.shape[0]
    p = lax.axis_index("row")
    c = lax.axis_index("col")
    rows = [[f0, f1, f2, f3], [g0, g1, g2, g3]]
    take_diagonal(p, c, facts[MASK], rows, diag, bsz)
    acc = update(facts, rows, [y, ya, yb, yc], coset_picks(facts[MASK]), y_all, link, bsz)
    mine = rhs[...] - acc[:bsz]
    pair = g0[:, 2 * bsz :] - acc[bsz:]
    t[:bsz] = mine
    t[bsz:] = pair
    y_mine, y_pair = solve_pair(facts, diag, 1, mine, pair)
    y1[:bsz] = y_mine
    y1[bsz:] = y_pair


def third_kernel(facts, f0, f1, f2, f3, g0, g1, g2, g3, y0, t, y, ya, yb, yc, out, diag, y_all, link):
    bsz = out.shape[0]
    p = lax.axis_index("row")
    c = lax.axis_index("col")
    rows = [[f0, f1, f2, f3], [g0, g1, g2, g3]]
    take_diagonal(p, c, facts[MASK], rows, diag, bsz)
    acc = update(facts, rows, [y, ya, yb, yc], coset_picks(facts[MASK]), y_all, link, bsz)
    y2, _ = solve_pair(facts, diag, 2, t[:bsz] - acc[:bsz], t[bsz:] - acc[bsz:])
    out[...] = y0[:bsz] + y[:bsz] + y2


def call(kernel, n_smem, args, outs, scratch):
    return pl.pallas_call(
        kernel,
        in_specs=[SMEM] * n_smem + [VMEM] * (len(args) - n_smem),
        out_specs=[spec for spec, _ in outs],
        out_shape=[shape for _, shape in outs],
        scratch_shapes=scratch,
        compiler_params=pltpu.CompilerParams(vmem_limit_bytes=32 * 1024 * 1024),
    )(*args)


def pair_body(factor, rhs, parent, bounds, slot, structure, n_row, n_col):
    bsz, wide = rhs.shape
    f32 = jnp.float32

    def send(value, row_mask, col_mask):
        pairs = [
            (r * n_col + k, (r ^ row_mask) * n_col + (k ^ col_mask)) for r in range(n_row) for k in range(n_col)
        ]
        return lax.ppermute(value, ("row", "col"), pairs)

    def array(*shape):
        return (VMEM, jax.ShapeDtypeStruct(shape, f32))

    f0 = factor
    f2 = send(f0, 0, 2)
    facts, packed = call(
        facts_kernel,
        4,
        [parent, bounds, slot, structure, factor, rhs],
        [(SMEM, jax.ShapeDtypeStruct((FACTS,), jnp.int32)), array(bsz, 2 * bsz + wide)],
        [pltpu.SMEM((8,), jnp.int32)],
    )
    m = facts[MASK]
    g0, g2 = lax.switch(
        m - 1,
        [lambda a, b, k=k: (send(a, k, 0), send(b, k, 2)) for k in range(1, n_row)],
        packed,
        f0,
    )
    f1, f3, g1, g3 = [send(v, 0, 1) for v in (f0, f2, g0, g2)]
    rows = [f0, f1, f2, f3, g0, g1, g2, g3]

    diag = pltpu.VMEM((2, 2, bsz, bsz), f32)
    y_all = pltpu.VMEM((n_row * bsz, wide), f32)
    link = pltpu.VMEM((2 * bsz, n_row * bsz), f32)

    variant = jnp.where(m >= 4, 0, jnp.where(m == 1, 1, 2))

    def spread(y):
        return lax.switch(
            variant,
            [lambda v, ks=ks: tuple(send(v, k, 0) for k in ks) for ks in ((1, 2, 3), (2, 4, 6), (1, 4, 5))],
            y,
        )

    (y0,) = call(first_kernel, 1, [facts, rhs] + rows, [array(2 * bsz, wide)], [diag])
    y1, t = call(
        second_kernel,
        1,
        [facts, rhs] + rows + [y0, *spread(y0)],
        [array(2 * bsz, wide), array(2 * bsz, wide)],
        [diag, y_all, link],
    )
    (out,) = call(
        third_kernel,
        1,
        [facts] + rows + [y0, t, y1, *spread(y1)],
        [array(bsz, wide)],
        [diag, y_all, link],
    )
    return out


def body(factor, rhs, parent, bounds, slot, structure, n_row, n_col):
    count = slot.shape[0]
    pairs = count == 8 and n_row == 8 and n_col == 4 and bounds.shape[0] == 8
    if pairs:
        return pair_body(factor, rhs, parent, bounds, slot, structure, n_row, n_col)
    return general_body(factor, rhs, parent, bounds, slot, structure, n_row)


def solution(mesh):
    in_specs = (P("row", "col"), P("row", "col"), P(), P(), P(), P())
    out_specs = P("row", "col")
    step = functools.partial(body, n_row=mesh.shape["row"], n_col=mesh.shape["col"])
    return jax.shard_map(step, mesh=mesh, in_specs=in_specs, out_specs=out_specs, check_vma=False)
```

time: 177 us -> 55.3 us (0.31)
  blocking collectives: 166 us -> 0 us
  waiting for transfers between devices: 0 us -> 27.3 us
  starting transfers between devices: 0 us -> 14.7 us
  Pallas kernels: 0 us -> 9.79 us
  matrix products: 4.68 us -> 0 us
  between operations: 2 us -> 0.18 us
    all_gather x6 -> x0, blocking collectives: 166 us -> none  [the longest x5 157 us: product(): lax.all_gather(vector, 'row', axis=0, tiled=True)]
    ppermute x0 -> x13, waiting for transfers between devices: none -> 27.3 us  [send(): return lax.ppermute(value, ('row', 'col'), pairs)]
    ppermute x0 -> x13, starting transfers between devices: none -> 14.7 us  [send(): return lax.ppermute(value, ('row', 'col'), pairs)]
    pallas_call x0 -> x4, Pallas kernels: none -> 9.79 us  [call(): pl.pallas_call(kernel, in_specs=[SMEM] * n_smem + [VMEM] * (len(args) - n...]
    dot_general x9 -> x0, matrix products: 4.68 us -> none  [the longest x5 3.93 us: product(): jnp.dot(matrix, lax.all_gather(vector, 'row', axis=0, tiled=True), precis...]
  transfers between devices with their start and end apart: 0 -> 13, of which waited for: 0 -> 7; matrix products, arithmetic and copies ran while one was open for 0% -> 0% of each run, Pallas kernels for 0% -> 3%
where the time goes in v1:
time: 55.3 us; the launch traced here: 55.5 us
  waiting for transfers between devices  27.3 us (49%)
  starting transfers between devices  14.7 us (27%)
  Pallas kernels  9.79 us (18%)
  local copies, waits for them, and re-layouts  3.5 us (6%)
    ppermute x13, waiting for transfers between devices, send(): return lax.ppermute(value, ('row', 'col'), pairs)  27.3 us
    ppermute x13, starting transfers between devices, send(): return lax.ppermute(value, ('row', 'col'), pairs)  14.7 us
    pallas_call x4, Pallas kernels, call(): pl.pallas_call(kernel, in_specs=[SMEM] * n_smem + [VMEM] * (len(args) - n...  9.79 us
    unnamed x14, local copies, waits for them, and re-layouts  3.5 us
  transfers between devices with their start and end apart: 13, of which 7 were waited for; matrix products, arithmetic and copies ran while one was open for 0% of the time, Pallas kernels for 3%

profile of v1, /device:TPU:0, one launch (start us, length us, event | category | flops | bytes accessed | tf_op | source)
XLA Modules:
  0.0 55.5 jit_solution(1145806545408232885)
XLA Ops:
  0.0 2.9 %collective-permute-start.33 = (f32[128,256]{1,0:T(8,128)}, f32[128,256]{1,0:T(8,128)S(1)}, u32[]{:S(2)}, u32[]{:S(2)}) collective-permute-start(f32[128,256]{1,0:T(8,128)} %f0.5), channel_id=1, source_target_pairs={{0,2},{1,3},{2,0},{3,1},{4,6},{5,7},{6,4},{7,5},{8,10},{9,11},{10,... | collective-permute-start | bytes 393224 | tf_op jit(solution)/shard_map/ppermute | solution.py:221
  2.9 0.8 %copy-done = f32[128,128]{1,0:T(8,128)S(1)} copy-done((f32[128,128]{1,0:T(8,128)S(1)}, f32[128,128]{1,0:T(8,128)}, u32[]{:S(2)}) %copy-start) | copy-done | bytes 65560
  3.8 0.7 %copy-done.2 = s32[7,8]{1,0:T(8,128)S(1)} copy-done((s32[7,8]{1,0:T(8,128)S(1)}, s32[7,8]{1,0:T(8,128)}, u32[]{:S(2)}) %copy-start.2) | copy-done | bytes 248
  4.5 0.7 %copy-done.3 = s32[7]{0:T(128)S(1)} copy-done((s32[7]{0:T(128)S(1)}, s32[7]{0:T(128)}, u32[]{:S(2)}) %copy-start.3) | copy-done | bytes 52
  5.1 0.7 %copy-done.4 = s32[8]{0:T(128)S(1)} copy-done((s32[8]{0:T(128)S(1)}, s32[8]{0:T(128)}, u32[]{:S(2)}) %copy-start.4) | copy-done | bytes 56
  5.8 0.7 %copy-done.5 = s32[8]{0:T(128)S(1)} copy-done((s32[8]{0:T(128)S(1)}, s32[8]{0:T(128)}, u32[]{:S(2)}) %copy-start.5) | copy-done | bytes 56
  6.4 1.7 %shard_map.64 = (s32[32]{0:T(128)S(1)}, f32[128,384]{1,0:T(8,128)S(1)}) custom-call(s32[7]{0:T(128)S(1)} %copy-done.3, s32[8]{0:T(128)S(1)} %copy-done.4, s32[8]{0:T(128)S(1)} %copy-done.5, s32[7,8]{1,0:T(8,128)S(1)} %copy-done.2, f32[128,256]{1,0:T(8,128)} %f0.5, f32[128,128]{1,0:T(8,128)S(1)} %copy-done), custom_call_target="tpu_custom_call" | custom-call | tf_op jit(solution)/shard_map/pallas_call | solution.py:203
  8.2 0.0 copy-start.1
  8.2 18.2 %conditional.3 = (f32[128,384]{1,0:T(8,128)}, f32[128,256]{1,0:T(8,128)}) conditional(s32[]{:T(128)} %bitcast, (f32[128,384]{1,0:T(8,128)S(1)}, f32[128,256]{1,0:T(8,128)S(1)}) %tuple.71, (f32[128,384]{1,0:T(8,128)S(1)}, f32[128,256]{1,0:T(8,128)S(1)}) %tuple.72, (f32[128,384]{1,0:T(8,128)S(1)}, ...), branch_computations={%region_0.0_spmd, %region_1.0_spmd, %region_2.0_spmd, %region_3.0_... | conditional | bytes 1310816 | solution.py:236
  8.3 3.6 %collective-permute-start.8 = (f32[128,384]{1,0:T(8,128)S(1)}, f32[128,384]{1,0:T(8,128)}, u32[]{:S(2)}, u32[]{:S(2)}) collective-permute-start(f32[128,384]{1,0:T(8,128)S(1)} %get-tuple-element.47), channel_id=1, source_target_pairs={{0,20},{1,21},{2,22},{3,23},{4,16},{5,17},{6,18},{7,19},{8,28},{9,... | collective-permute-start | bytes 589832 | tf_op jit(solution)/shard_map/cond/branch_4_fun/ppermute | solution.py:221
  11.9 0.1 collective-permute-start.9
  11.9 14.5 %collective-permute-done.9 = f32[128,256]{1,0:T(8,128)} collective-permute-done((f32[128,256]{1,0:T(8,128)S(1)}, f32[128,256]{1,0:T(8,128)}, u32[]{:S(2)}, u32[]{:S(2)}) %collective-permute-start.9) | collective-permute-done | bytes 131104 | tf_op jit(solution)/shard_map/cond/branch_4_fun/ppermute | solution.py:221
  26.5 0.5 collective-permute-start.32
  27.0 0.0 collective-permute-start.36
  27.0 0.5 collective-permute-start.34
  27.6 0.5 collective-permute-done.32.f1
  28.1 0.5 collective-permute-done.36.g3
  28.6 1.5 %shard_map.65.y.y0 = f32[256,128]{1,0:T(8,128)S(1)} custom-call(s32[32]{0:T(128)S(1)} %get-tuple-element.65.facts, f32[128,128]{1,0:T(8,128)S(1)} %copy-done.1, f32[128,256]{1,0:T(8,128)S(1)} %copy-done.6, f32[128,256]{1,0:T(8,128)S(1)} %collective-permute-done.32.f1, f32[128,256]{1,0:T(8,128)S(1)} %collective-permute-done.33.f2, ...), custom_call_target="tpu_custom_call" | custom-call | tf_op jit(solution)/shard_map/pallas_call | solution.py:203
  30.2 9.5 %conditional.4 = (f32[256,128]{1,0:T(8,128)}, f32[256,128]{1,0:T(8,128)}, f32[256,128]{1,0:T(8,128)}) conditional(s32[]{:T(128)} %bitcast.1, f32[256,128]{1,0:T(8,128)S(1)} %shard_map.65.y.y0, f32[256,128]{1,0:T(8,128)S(1)} %shard_map.65.y.y0, f32[256,128]{1,0:T(8,128)S(1)} %shard_map.65.y.y0), branch_computations={%region_7.8_spmd, %region_8.9_spmd, %region_9.10_spmd} | conditional | bytes 1573008 | solution.py:252
  30.2 0.5 collective-permute-start.16
  30.7 2.5 %collective-permute-start.15 = (f32[256,128]{1,0:T(8,128)S(1)}, f32[256,128]{1,0:T(8,128)}, u32[]{:S(2)}, u32[]{:S(2)}) collective-permute-start(f32[256,128]{1,0:T(8,128)S(1)} %param.7), channel_id=1, source_target_pairs={{0,8},{1,9},{2,10},{3,11},{4,12},{5,13},{6,14},{7,15},{8,0},{9,1},... | collective-permute-start | bytes 393224 | tf_op jit(solution)/shard_map/cond/branch_0_fun/ppermute | solution.py:221
  33.2 0.5 collective-permute-start.14
  33.8 3.9 %collective-permute-done.16 = f32[256,128]{1,0:T(8,128)} collective-permute-done((f32[256,128]{1,0:T(8,128)S(1)}, f32[256,128]{1,0:T(8,128)}, u32[]{:S(2)}, u32[]{:S(2)}) %collective-permute-start.16) | collective-permute-done | bytes 131104 | tf_op jit(solution)/shard_map/cond/branch_0_fun/ppermute | solution.py:221
  37.6 2.1 %collective-permute-done.15 = f32[256,128]{1,0:T(8,128)} collective-permute-done((f32[256,128]{1,0:T(8,128)S(1)}, f32[256,128]{1,0:T(8,128)}, u32[]{:S(2)}, u32[]{:S(2)}) %collective-permute-start.15) | collective-permute-done | bytes 131104 | tf_op jit(solution)/shard_map/cond/branch_0_fun/ppermute | solution.py:221
  39.7 3.1 %shard_map.66 = (f32[256,128]{1,0:T(8,128)S(1)}, f32[256,128]{1,0:T(8,128)S(1)}) custom-call(s32[32]{0:T(128)S(1)} %get-tuple-element.65.facts, f32[128,128]{1,0:T(8,128)S(1)} %copy-done.1, f32[128,256]{1,0:T(8,128)S(1)} %copy-done.6, f32[128,256]{1,0:T(8,128)S(1)} %collective-permute-done.32.f1, f32[128,256]{1,0:T(8,128)S(1)} %collective-permute-done.33.f2, ...), custom_call_target="tpu_custom_call" | custom-call | tf_op jit(solution)/shard_map/pallas_call | solution.py:203
  42.9 9.3 %conditional.5 = (f32[256,128]{1,0:T(8,128)}, f32[256,128]{1,0:T(8,128)}, f32[256,128]{1,0:T(8,128)}) conditional(s32[]{:T(128)} %bitcast.1, f32[256,128]{1,0:T(8,128)S(1)} %get-tuple-element.73.y, f32[256,128]{1,0:T(8,128)S(1)} %get-tuple-element.73.y, f32[256,128]{1,0:T(8,128)S(1)} %get-tuple-element.73.y), branch_computations={%region_10.11_spmd, %region_11.12_spmd, %region_12.13_spmd} | conditional | bytes 1573008 | solution.py:252
  42.9 0.6 %collective-permute-start.25 = (f32[256,128]{1,0:T(8,128)S(1)}, f32[256,128]{1,0:T(8,128)}, u32[]{:S(2)}, u32[]{:S(2)}) collective-permute-start(f32[256,128]{1,0:T(8,128)S(1)} %param.10), channel_id=1, source_target_pairs={{0,12},{1,13},{2,14},{3,15},{4,8},{5,9},{6,10},{7,11},{8,4},{9,5},... | collective-permute-start | bytes 393224 | tf_op jit(solution)/shard_map/cond/branch_0_fun/ppermute | solution.py:221
  43.5 2.4 %collective-permute-start.24 = (f32[256,128]{1,0:T(8,128)S(1)}, f32[256,128]{1,0:T(8,128)}, u32[]{:S(2)}, u32[]{:S(2)}) collective-permute-start(f32[256,128]{1,0:T(8,128)S(1)} %param.10), channel_id=1, source_target_pairs={{0,8},{1,9},{2,10},{3,11},{4,12},{5,13},{6,14},{7,15},{8,0},{9,1},... | collective-permute-start | bytes 393224 | tf_op jit(solution)/shard_map/cond/branch_0_fun/ppermute | solution.py:221
  45.9 0.6 %collective-permute-start.23 = (f32[256,128]{1,0:T(8,128)S(1)}, f32[256,128]{1,0:T(8,128)}, u32[]{:S(2)}, u32[]{:S(2)}) collective-permute-start(f32[256,128]{1,0:T(8,128)S(1)} %param.10), channel_id=1, source_target_pairs={{0,4},{1,5},{2,6},{3,7},{4,0},{5,1},{6,2},{7,3},{8,12},{9,13},{10,... | collective-permute-start | bytes 393224 | tf_op jit(solution)/shard_map/cond/branch_0_fun/ppermute | solution.py:221
  46.4 3.9 %collective-permute-done.25 = f32[256,128]{1,0:T(8,128)} collective-permute-done((f32[256,128]{1,0:T(8,128)S(1)}, f32[256,128]{1,0:T(8,128)}, u32[]{:S(2)}, u32[]{:S(2)}) %collective-permute-start.25) | collective-permute-done | bytes 131104 | tf_op jit(solution)/shard_map/cond/branch_0_fun/ppermute | solution.py:221
  50.4 1.8 %collective-permute-done.24 = f32[256,128]{1,0:T(8,128)} collective-permute-done((f32[256,128]{1,0:T(8,128)S(1)}, f32[256,128]{1,0:T(8,128)}, u32[]{:S(2)}, u32[]{:S(2)}) %collective-permute-start.24) | collective-permute-done | bytes 131104 | tf_op jit(solution)/shard_map/cond/branch_0_fun/ppermute | solution.py:221
  52.2 3.4 %shard_map.67 = f32[128,128]{1,0:T(8,128)} custom-call(s32[32]{0:T(128)S(1)} %get-tuple-element.65.facts, f32[128,256]{1,0:T(8,128)S(1)} %copy-done.6, f32[128,256]{1,0:T(8,128)S(1)} %collective-permute-done.32.f1, f32[128,256]{1,0:T(8,128)S(1)} %collective-permute-done.33.f2, f32[128,256]{1,0:T(8,128)S(1)} %collective-permute-done.34.f3, ...), custom_call_target="tpu_custom_call" | custom-call | tf_op jit(solution)/shard_map/pallas_call | solution.py:203
  (15 shorter events, 0.0 us)
Async XLA Ops:
  0.0 27.0 %collective-permute-start.33 = (f32[128,256]{1,0:T(8,128)}, f32[128,256]{1,0:T(8,128)S(1)}, u32[]{:S(2)}, u32[]{:S(2)}) collective-permute-start(f32[128,256]{1,0:T(8,128)} %f0.5), channel_id=1, source_target_pairs={{0,2},{1,3},{2,0},{3,1},{4,6},{5,7},{6,4},{7,5},{8,10},{9,11},{10,... | collective-permute-start | bytes 393224 | tf_op jit(solution)/shard_map/ppermute | solution.py:221
  2.9 0.8 %copy-start = (f32[128,128]{1,0:T(8,128)S(1)}, f32[128,128]{1,0:T(8,128)}, u32[]{:S(2)}) copy-start(f32[128,128]{1,0:T(8,128)} %rhs.5) | copy-start | bytes 196612
  3.8 0.7 %copy-start.2 = (s32[7,8]{1,0:T(8,128)S(1)}, s32[7,8]{1,0:T(8,128)}, u32[]{:S(2)}) copy-start(s32[7,8]{1,0:T(8,128)} %structure.1) | copy-start | bytes 676
  4.5 0.7 %copy-start.3 = (s32[7]{0:T(128)S(1)}, s32[7]{0:T(128)}, u32[]{:S(2)}) copy-start(s32[7]{0:T(128)} %parent.1) | copy-start | bytes 88
  5.1 0.7 %copy-start.4 = (s32[8]{0:T(128)S(1)}, s32[8]{0:T(128)}, u32[]{:S(2)}) copy-start(s32[8]{0:T(128)} %bounds.1) | copy-start | bytes 100
  5.8 0.7 %copy-start.5 = (s32[8]{0:T(128)S(1)}, s32[8]{0:T(128)}, u32[]{:S(2)}) copy-start(s32[8]{0:T(128)} %slot.1) | copy-start | bytes 100
  6.4 1.8 %copy-start.6 = (f32[128,256]{1,0:T(8,128)S(1)}, f32[128,256]{1,0:T(8,128)}, u32[]{:S(2)}) copy-start(f32[128,256]{1,0:T(8,128)} %f0.5) | copy-start | bytes 393220
  8.2 20.5 %copy-start.1 = (f32[128,128]{1,0:T(8,128)S(1)}, f32[128,128]{1,0:T(8,128)}, u32[]{:S(2)}) copy-start(f32[128,128]{1,0:T(8,128)} %rhs.5) | copy-start | bytes 196612
  8.3 18.2 %collective-permute-start.8 = (f32[128,384]{1,0:T(8,128)S(1)}, f32[128,384]{1,0:T(8,128)}, u32[]{:S(2)}, u32[]{:S(2)}) collective-permute-start(f32[128,384]{1,0:T(8,128)S(1)} %get-tuple-element.47), channel_id=1, source_target_pairs={{0,20},{1,21},{2,22},{3,23},{4,16},{5,17},{6,18},{7,19},{8,28},{9,... | collective-permute-start | bytes 589832 | tf_op jit(solution)/shard_map/cond/branch_4_fun/ppermute | solution.py:221
  11.9 14.6 %collective-permute-start.9 = (f32[128,256]{1,0:T(8,128)S(1)}, f32[128,256]{1,0:T(8,128)}, u32[]{:S(2)}, u32[]{:S(2)}) collective-permute-start(f32[128,256]{1,0:T(8,128)S(1)} %get-tuple-element.48), channel_id=1, source_target_pairs={{0,22},{1,23},{2,20},{3,21},{4,18},{5,19},{6,16},{7,17},{8,30},{9,... | collective-permute-start | bytes 393224 | tf_op jit(solution)/shard_map/cond/branch_4_fun/ppermute | solution.py:221
  26.5 2.2 %collective-permute-start.35 = (f32[128,384]{1,0:T(8,128)}, f32[128,384]{1,0:T(8,128)S(1)}, u32[]{:S(2)}, u32[]{:S(2)}) collective-permute-start(f32[128,384]{1,0:T(8,128)} %get-tuple-element.67.g0), channel_id=1, source_target_pairs={{0,1},{1,0},{2,3},{3,2},{4,5},{5,4},{6,7},{7,6},{8,9},{9,8},{10,11... | collective-permute-start | bytes 589832 | tf_op jit(solution)/shard_map/ppermute | solution.py:221
  26.5 1.6 %collective-permute-start.32 = (f32[128,256]{1,0:T(8,128)S(1)}, f32[128,256]{1,0:T(8,128)S(1)}, u32[]{:S(2)}, u32[]{:S(2)}) collective-permute-start(f32[128,256]{1,0:T(8,128)S(1)} %copy-done.6), channel_id=1, source_target_pairs={{0,1},{1,0},{2,3},{3,2},{4,5},{5,4},{6,7},{7,6},{8,9},{9,8},{10,11... | collective-permute-start | bytes 393224 | tf_op jit(solution)/shard_map/ppermute | solution.py:221
  27.0 1.7 %collective-permute-start.36 = (f32[128,256]{1,0:T(8,128)}, f32[128,256]{1,0:T(8,128)S(1)}, u32[]{:S(2)}, u32[]{:S(2)}) collective-permute-start(f32[128,256]{1,0:T(8,128)} %get-tuple-element.68.g2), channel_id=1, source_target_pairs={{0,1},{1,0},{2,3},{3,2},{4,5},{5,4},{6,7},{7,6},{8,9},{9,8},{10,11... | collective-permute-start | bytes 393224 | tf_op jit(solution)/shard_map/ppermute | solution.py:221
  27.0 1.7 %collective-permute-start.34 = (f32[128,256]{1,0:T(8,128)S(1)}, f32[128,256]{1,0:T(8,128)S(1)}, u32[]{:S(2)}, u32[]{:S(2)}) collective-permute-start(f32[128,256]{1,0:T(8,128)S(1)} %collective-permute-done.33.f2), channel_id=1, source_target_pairs={{0,1},{1,0},{2,3},{3,2},{4,5},{5,4},{6,7},{7,6},{8,9},{9,8},{10,11... | collective-permute-start | bytes 393224 | tf_op jit(solution)/shard_map/ppermute | solution.py:221
  30.2 7.4 %collective-permute-start.16 = (f32[256,128]{1,0:T(8,128)S(1)}, f32[256,128]{1,0:T(8,128)}, u32[]{:S(2)}, u32[]{:S(2)}) collective-permute-start(f32[256,128]{1,0:T(8,128)S(1)} %param.7), channel_id=1, source_target_pairs={{0,12},{1,13},{2,14},{3,15},{4,8},{5,9},{6,10},{7,11},{8,4},{9,5},... | collective-permute-start | bytes 393224 | tf_op jit(solution)/shard_map/cond/branch_0_fun/ppermute | solution.py:221
  30.7 9.0 %collective-permute-start.15 = (f32[256,128]{1,0:T(8,128)S(1)}, f32[256,128]{1,0:T(8,128)}, u32[]{:S(2)}, u32[]{:S(2)}) collective-permute-start(f32[256,128]{1,0:T(8,128)S(1)} %param.7), channel_id=1, source_target_pairs={{0,8},{1,9},{2,10},{3,11},{4,12},{5,13},{6,14},{7,15},{8,0},{9,1},... | collective-permute-start | bytes 393224 | tf_op jit(solution)/shard_map/cond/branch_0_fun/ppermute | solution.py:221
  33.2 6.5 %collective-permute-start.14 = (f32[256,128]{1,0:T(8,128)S(1)}, f32[256,128]{1,0:T(8,128)}, u32[]{:S(2)}, u32[]{:S(2)}) collective-permute-start(f32[256,128]{1,0:T(8,128)S(1)} %param.7), channel_id=1, source_target_pairs={{0,4},{1,5},{2,6},{3,7},{4,0},{5,1},{6,2},{7,3},{8,12},{9,13},{10,... | collective-permute-start | bytes 393224 | tf_op jit(solution)/shard_map/cond/branch_0_fun/ppermute | solution.py:221
  42.9 7.5 %collective-permute-start.25 = (f32[256,128]{1,0:T(8,128)S(1)}, f32[256,128]{1,0:T(8,128)}, u32[]{:S(2)}, u32[]{:S(2)}) collective-permute-start(f32[256,128]{1,0:T(8,128)S(1)} %param.10), channel_id=1, source_target_pairs={{0,12},{1,13},{2,14},{3,15},{4,8},{5,9},{6,10},{7,11},{8,4},{9,5},... | collective-permute-start | bytes 393224 | tf_op jit(solution)/shard_map/cond/branch_0_fun/ppermute | solution.py:221
  43.5 8.7 %collective-permute-start.24 = (f32[256,128]{1,0:T(8,128)S(1)}, f32[256,128]{1,0:T(8,128)}, u32[]{:S(2)}, u32[]{:S(2)}) collective-permute-start(f32[256,128]{1,0:T(8,128)S(1)} %param.10), channel_id=1, source_target_pairs={{0,8},{1,9},{2,10},{3,11},{4,12},{5,13},{6,14},{7,15},{8,0},{9,1},... | collective-permute-start | bytes 393224 | tf_op jit(solution)/shard_map/cond/branch_0_fun/ppermute | solution.py:221
  45.9 6.3 %collective-permute-start.23 = (f32[256,128]{1,0:T(8,128)S(1)}, f32[256,128]{1,0:T(8,128)}, u32[]{:S(2)}, u32[]{:S(2)}) collective-permute-start(f32[256,128]{1,0:T(8,128)S(1)} %param.10), channel_id=1, source_target_pairs={{0,4},{1,5},{2,6},{3,7},{4,0},{5,1},{6,2},{7,3},{8,12},{9,13},{10,... | collective-permute-start | bytes 393224 | tf_op jit(solution)/shard_map/cond/branch_0_fun/ppermute | solution.py:221

commit v2 on v0

v2 whole, which is shorter than its diff:
```python
import functools
import itertools

import jax
import jax.numpy as jnp
import numpy as np
from jax import lax
from jax.experimental import pallas as pl
from jax.experimental.pallas import tpu as pltpu
from jax.sharding import PartitionSpec as P

SMEM = pl.BlockSpec(memory_space=pltpu.SMEM)
VMEM = pl.BlockSpec(memory_space=pltpu.VMEM)
HIGHEST = lax.Precision.HIGHEST


def block_masks(parent, bounds, slot, structure):
    count = slot.shape[0]
    ar = jnp.arange(count, dtype=jnp.int32)
    logical = jnp.sum(jnp.where(slot[:, None] == ar[None, :], ar[:, None], 0), axis=0)
    node = jnp.sum((logical[:, None] >= bounds[None, 1:7]).astype(jnp.int32), axis=1)
    level = (node >= 4).astype(jnp.int32) + (node >= 6).astype(jnp.int32)
    nodes = jnp.arange(7, dtype=jnp.int32)
    grand = parent[parent]
    ancestor = ((nodes[None, :] == parent[:, None]) | (nodes[None, :] == grand[:, None])) & (
        nodes[None, :] != nodes[:, None]
    )
    node_hot = (node[:, None] == nodes[None, :]).astype(jnp.float32)
    perm_hot = (logical[:, None] == ar[None, :]).astype(jnp.float32)
    listed_store = jnp.dot(structure.astype(jnp.float32), perm_hot.T, precision=HIGHEST)
    anc_pairs = jnp.dot(
        node_hot, jnp.dot(ancestor.astype(jnp.float32), node_hot.T, precision=HIGHEST), precision=HIGHEST
    )
    list_pairs = jnp.dot(node_hot, listed_store, precision=HIGHEST)
    link = (anc_pairs * list_pairs).T > 0.5
    same = node[:, None] == node[None, :]
    return level, same, link


def masked(block_rows, mask):
    rblocks, width = mask.shape
    bsz = block_rows.shape[0] // rblocks
    shaped = block_rows.reshape(rblocks, bsz, width, bsz) * mask[:, None, :, None].astype(jnp.float32)
    return shaped.reshape(block_rows.shape)


def general_body(factor, rhs, parent, bounds, slot, structure, n_row):
    level, same, link = block_masks(parent, bounds, slot, structure)
    held = slot.shape[0] // n_row
    bsz = factor.shape[0] // held
    first = lax.axis_index("row") * held
    level_mine = lax.dynamic_slice_in_dim(level, first, held, 0)
    same_mine = lax.dynamic_slice_in_dim(same, first, held, 0)
    link_mine = lax.dynamic_slice_in_dim(link, first, held, 0)
    full_rows = lax.all_gather(factor, "col", axis=1, tiled=True)
    diag_part = masked(full_rows, same_mine)
    link_part = masked(full_rows, link_mine)

    def product(matrix, vector):
        return jnp.dot(
            matrix,
            lax.all_gather(vector, "row", axis=0, tiled=True),
            precision=HIGHEST,
            preferred_element_type=jnp.float32,
        )

    acc = jnp.zeros(rhs.shape, jnp.float32)
    result = jnp.zeros(rhs.shape, jnp.float32)
    for section in range(3):
        rows = jnp.repeat(level_mine == section, bsz)[:, None]
        solved = jnp.where(rows, product(diag_part, rhs - acc), 0.0)
        result = result + solved
        if section < 2:
            acc = acc + product(link_part, solved)
    return result


COUPLE = 0
SPREAD = 3
SAME = 4
LEVEL = 5
LINK0 = 8
LINK1 = 16
PICK = 20
FACTS = 24


def mask_sets():
    sets = [s for size in (2, 3) for s in itertools.combinations(range(1, 8), size)]
    sets += [s for s in itertools.combinations(range(1, 8), 4) if s[0] ^ s[1] ^ s[2] ^ s[3] == 0]
    table = np.zeros(256, np.int32)
    for i, s in enumerate(sets):
        table[sum(1 << k for k in s)] = i
    return sets, table


def as_int(flag):
    return jnp.where(flag, jnp.int32(1), jnp.int32(0))


def facts_kernel(parent_in, bounds_in, slot_in, structure_in, table_in, facts, parent, bounds, slot, structure, table, logical, node, sems):
    pairs = [(parent_in, parent), (bounds_in, bounds), (slot_in, slot), (structure_in, structure), (table_in, table)]
    copies = [pltpu.make_async_copy(a, b, sems.at[i]) for i, (a, b) in enumerate(pairs)]
    for copy in copies:
        copy.start()
    for copy in copies:
        copy.wait()
    p = lax.axis_index("row")
    c = lax.axis_index("col")
    wide = jnp.int32(0)
    for s in range(1, 7):
        wide = wide + as_int(bounds[s] == s)
    m = slot[wide] ^ slot[wide + 1]
    wide_level = as_int(wide >= 4) + as_int(wide >= 6)
    for i in range(8):
        q = slot[i]
        logical[q] = i
        node[q] = i - as_int(i > wide)
    for k in range(3):
        facts[COUPLE + k] = jnp.where(wide_level == k, m, 0)
    mine = node[p]
    facts[SAME] = as_int(node[p ^ m] == mine)
    level = as_int(mine >= 4) + as_int(mine >= 6)
    facts[LEVEL] = level
    place = logical[p]

    def linked(q):
        below = node[q]
        up = parent[below]
        top = parent[up]
        above = ((mine == up) | (mine == top)) & (mine != below)
        return as_int(above & (structure[below, place] == 1))

    for k in range(8):
        q = k ^ (2 * c)
        facts[LINK0 + k] = linked(q) * as_int(node[q] < 4)
    bits = jnp.int32(0)
    for i in range(4, 7):
        for j in range(6, 8):
            one = (node[slot[i]] >= 4) & (node[slot[i]] < 6)
            two = node[slot[j]] >= 6
            bits = bits | jnp.where(one & two, jnp.int32(1) << (slot[i] ^ slot[j]), 0)
    facts[SPREAD] = table[bits]
    for k in range(4):
        facts[PICK + k] = 0
        facts[LINK1 + k] = 0
    count = jnp.int32(0)
    for k in range(1, 8):
        on = (bits >> k) & 1
        at = jnp.minimum(count, 3)

        @pl.when(on == 1)
        def _(k=k, at=at):
            q = p ^ k
            facts[PICK + at] = k
            facts[LINK1 + at] = linked(q) * as_int((node[q] >= 4) & (node[q] < 6))

        count = count + on


def dot(a, b):
    return jnp.dot(a, b, precision=HIGHEST, preferred_element_type=jnp.float32)


def solve(facts, diag, section, mine, partner):
    same = facts[SAME].astype(jnp.float32)
    on = (facts[LEVEL] == section).astype(jnp.float32)
    return (dot(diag[0], mine) + same * dot(diag[1], partner)) * on


def partner_mask(facts):
    return facts[COUPLE] + facts[COUPLE + 1] + facts[COUPLE + 2]


def first_kernel(facts, rhs, partner, f0, f1, f2, f3, y, diag):
    bsz = rhs.shape[0]
    p = lax.axis_index("row")
    c = lax.axis_index("col")
    pieces = [f0, f1, f2, f3]
    for s in range(2):
        place = p ^ (2 * c)
        if s == 1:
            place = place ^ partner_mask(facts)
        for k in range(8):

            @pl.when(place == k)
            def _(s=s, k=k):
                at = (k % 2) * bsz
                diag[s] = pieces[k // 2][:, at : at + bsz]

    y[...] = solve(facts, diag, 0, rhs[...], partner[...])


def residual(facts, rhs, f0, f1, f2, f3, ys, y_all, link):
    bsz = rhs.shape[0]
    p = lax.axis_index("row")
    c = lax.axis_index("col")
    pieces = [f0, f1, f2, f3]
    for k, y in enumerate(ys):
        place = p ^ k ^ (2 * c)
        y_all[pl.ds(pl.multiple_of(place * bsz, bsz), bsz), :] = y[...]
    for k in range(8):
        at = (k % 2) * bsz
        on = facts[LINK0 + k].astype(jnp.float32)
        link[:, k * bsz : (k + 1) * bsz] = pieces[k // 2][:, at : at + bsz] * on
    return rhs[...] - dot(link[...], y_all[...])


def second_kernel(facts, rhs, f0, f1, f2, f3, diag, *rest):
    ys, (t, y, y_all, link) = rest[:8], rest[8:]
    t[...] = residual(facts, rhs, f0, f1, f2, f3, ys, y_all, link)
    y[...] = solve(facts, diag, 1, t[...], t[...])


def residual_kernel(facts, rhs, f0, f1, f2, f3, *rest):
    ys, (t, y_all, link) = rest[:8], rest[8:]
    t[...] = residual(facts, rhs, f0, f1, f2, f3, ys, y_all, link)


def solve_kernel(facts, diag, t, partner, y):
    y[...] = solve(facts, diag, 1, t[...], partner[...])


def last_residual(facts, f0, f1, f2, f3, t, ys, total, block):
    bsz = t.shape[0]
    p = lax.axis_index("row")
    c = lax.axis_index("col")
    pieces = [f0, f1, f2, f3]
    total[...] = t[...]
    for s, y in enumerate(ys):

        @pl.when(facts[LINK1 + s] == 1)
        def _(s=s, y=y):
            place = p ^ facts[PICK + s] ^ (2 * c)
            for k in range(8):

                @pl.when(place == k)
                def _(k=k):
                    at = (k % 2) * bsz
                    block[...] = pieces[k // 2][:, at : at + bsz]

            total[...] -= dot(block[...], y[...])


def third_kernel(facts, f0, f1, f2, f3, diag, t, y0, y1, z0, z1, z2, z3, out, total, block):
    last_residual(facts, f0, f1, f2, f3, t, [z0, z1, z2, z3], total, block)
    out[...] = y0[...] + y1[...] + solve(facts, diag, 2, total[...], total[...])


def last_residual_kernel(facts, f0, f1, f2, f3, t, z0, z1, z2, z3, total, block):
    last_residual(facts, f0, f1, f2, f3, t, [z0, z1, z2, z3], total, block)


def last_solve_kernel(facts, diag, t, partner, y0, y1, out):
    out[...] = y0[...] + y1[...] + solve(facts, diag, 2, t[...], partner[...])


def call(kernel, args, outs, scratch=()):
    return pl.pallas_call(
        kernel,
        in_specs=[SMEM] + [VMEM] * (len(args) - 1),
        out_specs=[VMEM] * len(outs),
        out_shape=[jax.ShapeDtypeStruct(shape, jnp.float32) for shape in outs],
        scratch_shapes=[pltpu.VMEM(shape, jnp.float32) for shape in scratch],
        compiler_params=pltpu.CompilerParams(vmem_limit_bytes=32 * 1024 * 1024),
    )(*args)


def find_facts(parent, bounds, slot, structure, table):
    i32 = jnp.int32
    args = [parent, bounds, slot, structure, jnp.asarray(table)]
    return pl.pallas_call(
        facts_kernel,
        in_specs=[pl.BlockSpec(memory_space=pl.ANY)] * 5,
        out_specs=SMEM,
        out_shape=jax.ShapeDtypeStruct((FACTS,), i32),
        scratch_shapes=[pltpu.SMEM(a.shape, i32) for a in args]
        + [pltpu.SMEM((8,), i32), pltpu.SMEM((8,), i32), pltpu.SemaphoreType.DMA((5,))],
    )(*args)


def wide_body(factor, rhs, parent, bounds, slot, structure, n_row, n_col):
    bsz, cols = rhs.shape
    block = (bsz, cols)
    square = (bsz, bsz)
    sets, table = mask_sets()

    def send(value, row_mask, col_mask=0):
        pairs = [
            (r * n_col + k, (r ^ row_mask) * n_col + (k ^ col_mask)) for r in range(n_row) for k in range(n_col)
        ]
        return lax.ppermute(value, ("row", "col"), pairs)

    facts = find_facts(parent, bounds, slot, structure, table)

    def before(factor, rhs, mask):
        f2 = send(factor, 0, 2)
        partner = send(rhs, mask) if mask else rhs
        f1 = send(factor, 0, 1)
        f3 = send(f2, 0, 1)
        return f1, f2, f3, partner

    f1, f2, f3, partner = lax.switch(
        facts[COUPLE], [functools.partial(before, mask=k) for k in range(n_row)], factor, rhs
    )
    rows = [factor, f1, f2, f3]
    y0, diag = call(first_kernel, [facts, rhs, partner] + rows, [block, (2, bsz, bsz)])

    far = send(y0, 4)
    near = [send(y0, k) for k in (1, 2, 3)]
    ys = [y0] + near + [far] + [send(far, k) for k in (1, 2, 3)]

    def middle(mask, *args):
        facts, rhs, f0, f1, f2, f3, diag, *ys = args
        wide = (bsz, n_row * bsz)
        tall = (n_row * bsz, cols)
        if not mask:
            return tuple(call(second_kernel, args, [block, block], [tall, wide]))
        (t,) = call(residual_kernel, [facts, rhs, f0, f1, f2, f3] + ys, [block], [tall, wide])
        (y,) = call(solve_kernel, [facts, diag, t, send(t, mask)], [block])
        return t, y

    t, y1 = lax.switch(
        facts[COUPLE + 1],
        [functools.partial(middle, k) for k in range(n_row)],
        *([facts, rhs] + rows + [diag] + ys),
    )

    def spread(masks, y):
        return tuple(send(y, k) for k in masks) + (y,) * (4 - len(masks))

    zs = lax.switch(facts[SPREAD], [functools.partial(spread, s) for s in sets], y1)

    def end(mask, *args):
        facts, f0, f1, f2, f3, diag, t, y0, y1, *zs = args
        if not mask:
            return call(third_kernel, args, [block], [block, square])[0]
        (t2,) = call(last_residual_kernel, [facts, f0, f1, f2, f3, t] + zs, [block], [square])
        return call(last_solve_kernel, [facts, diag, t2, send(t2, mask), y0, y1], [block])[0]

    return lax.switch(
        facts[COUPLE + 2],
        [functools.partial(end, k) for k in range(n_row)],
        *([facts] + rows + [diag, t, y0, y1, *zs]),
    )


def body(factor, rhs, parent, bounds, slot, structure, n_row, n_col):
    count = slot.shape[0]
    if count == 8 and n_row == 8 and n_col == 4 and bounds.shape[0] == 8:
        return wide_body(factor, rhs, parent, bounds, slot, structure, n_row, n_col)
    return general_body(factor, rhs, parent, bounds, slot, structure, n_row)


def solution(mesh):
    in_specs = (P("row", "col"), P("row", "col"), P(), P(), P(), P())
    out_specs = P("row", "col")
    step = functools.partial(body, n_row=mesh.shape["row"], n_col=mesh.shape["col"])
    return jax.shard_map(step, mesh=mesh, in_specs=in_specs, out_specs=out_specs, check_vma=False)
```

time: 177 us -> 44.8 us (0.25)
  blocking collectives: 166 us -> 0 us
  starting transfers between devices: 0 us -> 18.3 us
  waiting for transfers between devices: 0 us -> 12.5 us
  Pallas kernels: 0 us -> 7.68 us
  matrix products: 4.68 us -> 0 us
    all_gather x6 -> x0, blocking collectives: 166 us -> none  [the longest x5 157 us: product(): lax.all_gather(vector, 'row', axis=0, tiled=True)]
    ppermute x0 -> x13, starting transfers between devices: none -> 18.3 us  [send(): return lax.ppermute(value, ('row', 'col'), pairs)]
    ppermute x0 -> x13, waiting for transfers between devices: none -> 12.5 us  [send(): return lax.ppermute(value, ('row', 'col'), pairs)]
    pallas_call x0 -> x4, Pallas kernels: none -> 7.68 us  [the longest x3 6.07 us: call(): pl.pallas_call(kernel, in_specs=[SMEM] + [VMEM] * (len(args) - 1), out_sp...]
    dot_general x9 -> x0, matrix products: 4.68 us -> none  [the longest x5 3.93 us: product(): jnp.dot(matrix, lax.all_gather(vector, 'row', axis=0, tiled=True), precis...]
    cond x0 -> x3, local copies, waits for them, and re-layouts: none -> 2.08 us
  transfers between devices with their start and end apart: 0 -> 13, of which waited for: 0 -> 6; matrix products, arithmetic and copies ran while one was open for 0% -> 3% of each run, Pallas kernels for 0% -> 0%
where the time goes in v2:
time: 44.8 us
  starting transfers between devices  18.3 us (41%)
  waiting for transfers between devices  12.5 us (28%)
  Pallas kernels  7.68 us (17%)
  local copies, waits for them, and re-layouts  3.36 us (8%)
  between operations  2.63 us (6%)
    ppermute x13, starting transfers between devices, send(): return lax.ppermute(value, ('row', 'col'), pairs)  18.3 us
    ppermute x13, waiting for transfers between devices, send(): return lax.ppermute(value, ('row', 'col'), pairs)  12.5 us
    pallas_call x3, Pallas kernels, call(): pl.pallas_call(kernel, in_specs=[SMEM] + [VMEM] * (len(args) - 1), out_sp...  6.07 us
    cond x3, local copies, waits for them, and re-layouts  2.08 us
    pallas_call x1, Pallas kernels, find_facts(): pl.pallas_call(facts_kernel, in_specs=[pl.BlockSpec(memory_space=pl.ANY)]...  1.61 us
  transfers between devices with their start and end apart: 13, of which 6 were waited for; matrix products, arithmetic and copies ran while one was open for 3% of the time, Pallas kernels for 0%

profile of v2, /device:TPU:0, one launch (start us, length us, event | category | flops | bytes accessed | tf_op | source)
XLA Modules:
  0.0 44.8 jit_solution(2023684739333562904)
XLA Ops:
  0.0 1.6 %shard_map.81.facts = s32[24]{0:T(128)S(1)} custom-call(s32[7]{0:T(128)} %parent_in.1, s32[8]{0:T(128)} %bounds_in.1, s32[8]{0:T(128)} %slot_in.1, s32[7,8]{1,0:T(8,128)} %structure_in.1, s32[256]{0:T(256)} %constant.16.clone.table_in), custom_call_target="tpu_custom_call" | custom-call | tf_op jit(solution)/shard_map/pallas_call | solution.py:272
  1.6 0.6 %fusion = (s32[1]{0:T(128)}, s32[1]{0:T(128)}, s32[1]{0:T(128)}, s32[1]{0:T(128)}) fusion(s32[24]{0:T(128)S(1)} %shard_map.81.facts), kind=kLoop, calls=%fused_computation | loop fusion | bytes 32 | tf_op jit(solution)/shard_map/slice | solution.py:332
  2.9 11.7 %conditional.4 = (f32[128,256]{1,0:T(8,128)}, f32[128,256]{1,0:T(8,128)}, f32[128,256]{1,0:T(8,128)}, f32[128,128]{1,0:T(8,128)}) conditional(s32[]{:T(128)} %bitcast.1, (f32[128,256]{1,0:T(8,128)}, f32[128,128]{1,0:T(8,128)}) %tuple.361, (f32[128,256]{1,0:T(8,128)}, f32[128,128]{1,0:T(8,128)}) %tuple.361, ...), branch_computations={%region_0.0_spmd, %region_1.0_spmd, %region_2.0_spmd, %region_3.0_... | conditional | bytes 1835200 | solution.py:303
  2.9 3.0 %collective-permute-start.4 = (f32[128,256]{1,0:T(8,128)}, f32[128,256]{1,0:T(8,128)}, u32[]{:S(2)}, u32[]{:S(2)}) collective-permute-start(f32[128,256]{1,0:T(8,128)} %get-tuple-element.562), channel_id=1, source_target_pairs={{0,2},{1,3},{2,0},{3,1},{4,6},{5,7},{6,4},{7,5},{8,10},{9,11},{10,... | collective-permute-start | bytes 393224 | tf_op jit(solution)/shard_map/cond/branch_1_fun/ppermute | solution.py:292
  5.9 3.8 %collective-permute-done.4 = f32[128,256]{1,0:T(8,128)} collective-permute-done((f32[128,256]{1,0:T(8,128)}, f32[128,256]{1,0:T(8,128)}, u32[]{:S(2)}, u32[]{:S(2)}) %collective-permute-start.4) | collective-permute-done | bytes 131104 | tf_op jit(solution)/shard_map/cond/branch_1_fun/ppermute | solution.py:292
  9.8 0.0 collective-permute-start.5
  9.8 1.8 %collective-permute-start.6 = (f32[128,128]{1,0:T(8,128)}, f32[128,128]{1,0:T(8,128)}, u32[]{:S(2)}, u32[]{:S(2)}) collective-permute-start(f32[128,128]{1,0:T(8,128)} %get-tuple-element.563), channel_id=1, source_target_pairs={{0,4},{1,5},{2,6},{3,7},{4,0},{5,1},{6,2},{7,3},{8,12},{9,13},{10,... | collective-permute-start | bytes 196616 | tf_op jit(solution)/shard_map/cond/branch_1_fun/ppermute | solution.py:292
  11.5 3.1 %collective-permute-done.6 = f32[128,128]{1,0:T(8,128)} collective-permute-done((f32[128,128]{1,0:T(8,128)}, f32[128,128]{1,0:T(8,128)}, u32[]{:S(2)}, u32[]{:S(2)}) %collective-permute-start.6) | collective-permute-done | bytes 65568 | tf_op jit(solution)/shard_map/cond/branch_1_fun/ppermute | solution.py:292
  14.6 0.0 copy-start.1
  14.6 1.6 %shard_map.82 = (f32[128,128]{1,0:T(8,128)S(1)}, f32[2,128,128]{2,1,0:T(8,128)S(1)}) custom-call(s32[24]{0:T(128)S(1)} %shard_map.81.facts, f32[128,128]{1,0:T(8,128)} %rhs.1, f32[128,128]{1,0:T(8,128)} %get-tuple-element.818.partner, f32[128,256]{1,0:T(8,128)} %f0.1, f32[128,256]{1,0:T(8,128)} %get-tuple-element.815.f1, f32[128,256]{1,0:T(8,128)} %get-tuple-element.816.f2, ...), custom_call_target="tpu_custom_call" | custom-call | tf_op jit(solution)/shard_map/pallas_call | solution.py:259
  16.2 2.9 %collective-permute-start.223 = (f32[128,128]{1,0:T(8,128)S(1)}, f32[128,128]{1,0:T(8,128)S(1)}, u32[]{:S(2)}, u32[]{:S(2)}) collective-permute-start(f32[128,128]{1,0:T(8,128)S(1)} %get-tuple-element.820), channel_id=1, source_target_pairs={{0,16},{1,17},{2,18},{3,19},{4,20},{5,21},{6,22},{7,23},{8,24},{9,... | collective-permute-start | bytes 196616 | tf_op jit(solution)/shard_map/ppermute | solution.py:292
  19.1 2.5 %collective-permute-start.222 = (f32[128,128]{1,0:T(8,128)S(1)}, f32[128,128]{1,0:T(8,128)S(1)}, u32[]{:S(2)}, u32[]{:S(2)}) collective-permute-start(f32[128,128]{1,0:T(8,128)S(1)} %get-tuple-element.820), channel_id=1, source_target_pairs={{0,12},{1,13},{2,14},{3,15},{4,8},{5,9},{6,10},{7,11},{8,4},{9,5},... | collective-permute-start | bytes 196616 | tf_op jit(solution)/shard_map/ppermute | solution.py:292
  21.6 0.5 %collective-permute-start.221 = (f32[128,128]{1,0:T(8,128)S(1)}, f32[128,128]{1,0:T(8,128)S(1)}, u32[]{:S(2)}, u32[]{:S(2)}) collective-permute-start(f32[128,128]{1,0:T(8,128)S(1)} %get-tuple-element.820), channel_id=1, source_target_pairs={{0,8},{1,9},{2,10},{3,11},{4,12},{5,13},{6,14},{7,15},{8,0},{9,1},... | collective-permute-start | bytes 196616 | tf_op jit(solution)/shard_map/ppermute | solution.py:292
  22.1 0.5 %collective-permute-start.220 = (f32[128,128]{1,0:T(8,128)S(1)}, f32[128,128]{1,0:T(8,128)S(1)}, u32[]{:S(2)}, u32[]{:S(2)}) collective-permute-start(f32[128,128]{1,0:T(8,128)S(1)} %get-tuple-element.820), channel_id=1, source_target_pairs={{0,4},{1,5},{2,6},{3,7},{4,0},{5,1},{6,2},{7,3},{8,12},{9,13},{10,... | collective-permute-start | bytes 196616 | tf_op jit(solution)/shard_map/ppermute | solution.py:292
  22.6 2.5 %collective-permute-start.226 = (f32[128,128]{1,0:T(8,128)S(1)}, f32[128,128]{1,0:T(8,128)S(1)}, u32[]{:S(2)}, u32[]{:S(2)}) collective-permute-start(f32[128,128]{1,0:T(8,128)S(1)} %collective-permute-done.223), channel_id=1, source_target_pairs={{0,12},{1,13},{2,14},{3,15},{4,8},{5,9},{6,10},{7,11},{8,4},{9,5},... | collective-permute-start | bytes 196616 | tf_op jit(solution)/shard_map/ppermute | solution.py:292
  25.1 0.5 %collective-permute-start.225 = (f32[128,128]{1,0:T(8,128)S(1)}, f32[128,128]{1,0:T(8,128)S(1)}, u32[]{:S(2)}, u32[]{:S(2)}) collective-permute-start(f32[128,128]{1,0:T(8,128)S(1)} %collective-permute-done.223), channel_id=1, source_target_pairs={{0,8},{1,9},{2,10},{3,11},{4,12},{5,13},{6,14},{7,15},{8,0},{9,1},... | collective-permute-start | bytes 196616 | tf_op jit(solution)/shard_map/ppermute | solution.py:292
  25.6 0.7 %collective-permute-start.224 = (f32[128,128]{1,0:T(8,128)S(1)}, f32[128,128]{1,0:T(8,128)S(1)}, u32[]{:S(2)}, u32[]{:S(2)}) collective-permute-start(f32[128,128]{1,0:T(8,128)S(1)} %collective-permute-done.223), channel_id=1, source_target_pairs={{0,4},{1,5},{2,6},{3,7},{4,0},{5,1},{6,2},{7,3},{8,12},{9,13},{10,... | collective-permute-start | bytes 196616 | tf_op jit(solution)/shard_map/ppermute | solution.py:292
  28.2 1.2 %collective-permute-done.225 = f32[128,128]{1,0:T(8,128)S(1)} collective-permute-done((f32[128,128]{1,0:T(8,128)S(1)}, f32[128,128]{1,0:T(8,128)S(1)}, u32[]{:S(2)}, u32[]{:S(2)}) %collective-permute-start.225) | collective-permute-done | bytes 65568 | tf_op jit(solution)/shard_map/ppermute | solution.py:292
  29.4 0.5 %collective-permute-done.224 = f32[128,128]{1,0:T(8,128)S(1)} collective-permute-done((f32[128,128]{1,0:T(8,128)S(1)}, f32[128,128]{1,0:T(8,128)S(1)}, u32[]{:S(2)}, u32[]{:S(2)}) %collective-permute-start.224) | collective-permute-done | bytes 65568 | tf_op jit(solution)/shard_map/ppermute | solution.py:292
  29.8 3.4 %conditional.5 = (f32[128,128]{1,0:T(8,128)}, f32[128,128]{1,0:T(8,128)}, f32[128,128]{1,0:T(8,128)S(1)}) conditional(s32[]{:T(128)} %bitcast.2, (s32[24]{0:T(128)S(1)}, f32[128,128]{1,0:T(8,128)S(1)}, f32[128,256]{1,0:T(8,128)S(1)}, f32[128,256]{1,0:T(8,128)}, f32[128,256]{1,0:T(8,128)}, ...), branch_computations={%region_8.0_spmd, %region_9.0_spmd, %region_10.0_spmd, %region_11.... | conditional | bytes 393280 | solution.py:323
  29.8 2.6 %branch_0_fun.2 = (f32[128,128]{1,0:T(8,128)}, f32[128,128]{1,0:T(8,128)}) custom-call(s32[24]{0:T(128)S(1)} %get-tuple-element.576.facts, f32[128,128]{1,0:T(8,128)S(1)} %get-tuple-element.577.rhs, f32[128,256]{1,0:T(8,128)S(1)} %get-tuple-element.578.f0, f32[128,256]{1,0:T(8,128)} %get-tuple-element.579.f1, f32[128,256]{1,0:T(8,128)} %get-tuple-element.580.f2, ...), custom_call_target="tpu_custom_call" | custom-call | tf_op jit(solution)/shard_map/cond/branch_0_fun/pallas_call | solution.py:259
  32.4 0.8 %copy.50 = f32[128,128]{1,0:T(8,128)S(1)} copy(f32[128,128]{1,0:T(8,128)} %get-tuple-element.867) | data formatting | bytes 131072 | tf_op jit(solution)/shard_map/cond
  33.2 8.7 %conditional.6 = (f32[128,128]{1,0:T(8,128)}, f32[128,128]{1,0:T(8,128)}, f32[128,128]{1,0:T(8,128)}, f32[128,128]{1,0:T(8,128)}) conditional(s32[]{:T(128)} %bitcast.3, f32[128,128]{1,0:T(8,128)S(1)} %get-tuple-element.823, f32[128,128]{1,0:T(8,128)S(1)} %get-tuple-element.823, ...), branch_computations={%region_16.0_spmd, %region_17.0_spmd, %region_18.0_spmd, %region_1... | conditional | bytes 1048768 | solution.py:332
  33.2 3.5 %collective-permute-start.73 = (f32[128,128]{1,0:T(8,128)S(1)}, f32[128,128]{1,0:T(8,128)}, u32[]{:S(2)}, u32[]{:S(2)}) collective-permute-start(f32[128,128]{1,0:T(8,128)S(1)} %param.33), channel_id=1, source_target_pairs={{0,28},{1,29},{2,30},{3,31},{4,24},{5,25},{6,26},{7,27},{8,20},{9,... | collective-permute-start | bytes 196616 | tf_op jit(solution)/shard_map/cond/branch_17_fun/ppermute | solution.py:292
  36.7 0.6 %copy.142 = f32[128,128]{1,0:T(8,128)} copy(f32[128,128]{1,0:T(8,128)S(1)} %param.33) | data formatting | bytes 131072 | tf_op jit(solution)/shard_map/cond
  37.3 0.6 %copy.143 = f32[128,128]{1,0:T(8,128)} copy(f32[128,128]{1,0:T(8,128)S(1)} %param.33) | data formatting | bytes 131072 | tf_op jit(solution)/shard_map/cond
  37.9 2.5 %collective-permute-done.73 = f32[128,128]{1,0:T(8,128)} collective-permute-done((f32[128,128]{1,0:T(8,128)S(1)}, f32[128,128]{1,0:T(8,128)}, u32[]{:S(2)}, u32[]{:S(2)}) %collective-permute-start.73) | collective-permute-done | bytes 65568 | tf_op jit(solution)/shard_map/cond/branch_17_fun/ppermute | solution.py:292
  40.4 1.6 %collective-permute-done.72 = f32[128,128]{1,0:T(8,128)} collective-permute-done((f32[128,128]{1,0:T(8,128)S(1)}, f32[128,128]{1,0:T(8,128)}, u32[]{:S(2)}, u32[]{:S(2)}) %collective-permute-start.72) | collective-permute-done | bytes 65568 | tf_op jit(solution)/shard_map/cond/branch_17_fun/ppermute | solution.py:292
  42.0 2.2 %conditional.7 = (f32[128,128]{1,0:T(8,128)S(1)}) conditional(s32[]{:T(128)} %bitcast, (s32[24]{0:T(128)S(1)}, f32[128,256]{1,0:T(8,128)S(1)}, f32[128,256]{1,0:T(8,128)}, f32[128,256]{1,0:T(8,128)}, f32[128,256]{1,0:T(8,128)}, /*index=5*/f32[2,128,128]{2,1,0:T(8,128)S(1)}, f32[128,128]{1,0:T(8,128)}, ...), branch_computations={%region_79.0_spmd, %region_80.0_spmd, %region_81.0_spmd, %region_8... | conditional | bytes 262192 | solution.py:341
  42.0 1.9 %branch_0_fun.3 = f32[128,128]{1,0:T(8,128)S(1)} custom-call(s32[24]{0:T(128)S(1)} %get-tuple-element.698.facts, f32[128,256]{1,0:T(8,128)S(1)} %get-tuple-element.699.f0, f32[128,256]{1,0:T(8,128)} %get-tuple-element.700.f1, f32[128,256]{1,0:T(8,128)} %get-tuple-element.701.f2, f32[128,256]{1,0:T(8,128)} %get-tuple-element.702.f3, ...), custom_call_target="tpu_custom_call" | custom-call | tf_op jit(solution)/shard_map/cond/branch_0_fun/pallas_call | solution.py:259
  44.2 0.0 copy-start.2
  44.2 0.6 %copy-done.2 = f32[128,128]{1,0:T(8,128)} copy-done((f32[128,128]{1,0:T(8,128)}, f32[128,128]{1,0:T(8,128)S(1)}, u32[]{:S(2)}) %copy-start.2) | copy-done | bytes 65560
  (12 shorter events, 0.0 us)
Async XLA Ops:
  2.9 6.8 %collective-permute-start.4 = (f32[128,256]{1,0:T(8,128)}, f32[128,256]{1,0:T(8,128)}, u32[]{:S(2)}, u32[]{:S(2)}) collective-permute-start(f32[128,256]{1,0:T(8,128)} %get-tuple-element.562), channel_id=1, source_target_pairs={{0,2},{1,3},{2,0},{3,1},{4,6},{5,7},{6,4},{7,5},{8,10},{9,11},{10,... | collective-permute-start | bytes 393224 | tf_op jit(solution)/shard_map/cond/branch_1_fun/ppermute | solution.py:292
  5.9 8.7 %collective-permute-start.3 = (f32[128,256]{1,0:T(8,128)}, f32[128,256]{1,0:T(8,128)}, u32[]{:S(2)}, u32[]{:S(2)}) collective-permute-start(f32[128,256]{1,0:T(8,128)} %get-tuple-element.562), channel_id=1, source_target_pairs={{0,1},{1,0},{2,3},{3,2},{4,5},{5,4},{6,7},{7,6},{8,9},{9,8},{10,11... | collective-permute-start | bytes 393224 | tf_op jit(solution)/shard_map/cond/branch_1_fun/ppermute | solution.py:292
  9.8 4.9 %collective-permute-start.5 = (f32[128,256]{1,0:T(8,128)}, f32[128,256]{1,0:T(8,128)}, u32[]{:S(2)}, u32[]{:S(2)}) collective-permute-start(f32[128,256]{1,0:T(8,128)} %collective-permute-done.4), channel_id=1, source_target_pairs={{0,1},{1,0},{2,3},{3,2},{4,5},{5,4},{6,7},{7,6},{8,9},{9,8},{10,11... | collective-permute-start | bytes 393224 | tf_op jit(solution)/shard_map/cond/branch_1_fun/ppermute | solution.py:292
  9.8 4.8 %collective-permute-start.6 = (f32[128,128]{1,0:T(8,128)}, f32[128,128]{1,0:T(8,128)}, u32[]{:S(2)}, u32[]{:S(2)}) collective-permute-start(f32[128,128]{1,0:T(8,128)} %get-tuple-element.563), channel_id=1, source_target_pairs={{0,4},{1,5},{2,6},{3,7},{4,0},{5,1},{6,2},{7,3},{8,12},{9,13},{10,... | collective-permute-start | bytes 196616 | tf_op jit(solution)/shard_map/cond/branch_1_fun/ppermute | solution.py:292
  14.6 15.2 %copy-start = (f32[128,256]{1,0:T(8,128)S(1)}, f32[128,256]{1,0:T(8,128)}, u32[]{:S(2)}) copy-start(f32[128,256]{1,0:T(8,128)} %f0.1) | copy-start | bytes 393220
  14.6 15.2 %copy-start.1 = (f32[128,128]{1,0:T(8,128)S(1)}, f32[128,128]{1,0:T(8,128)}, u32[]{:S(2)}) copy-start(f32[128,128]{1,0:T(8,128)} %rhs.1) | copy-start | bytes 196612
  16.2 6.4 %collective-permute-start.223 = (f32[128,128]{1,0:T(8,128)S(1)}, f32[128,128]{1,0:T(8,128)S(1)}, u32[]{:S(2)}, u32[]{:S(2)}) collective-permute-start(f32[128,128]{1,0:T(8,128)S(1)} %get-tuple-element.820), channel_id=1, source_target_pairs={{0,16},{1,17},{2,18},{3,19},{4,20},{5,21},{6,22},{7,23},{8,24},{9,... | collective-permute-start | bytes 196616 | tf_op jit(solution)/shard_map/ppermute | solution.py:292
  19.1 6.5 %collective-permute-start.222 = (f32[128,128]{1,0:T(8,128)S(1)}, f32[128,128]{1,0:T(8,128)S(1)}, u32[]{:S(2)}, u32[]{:S(2)}) collective-permute-start(f32[128,128]{1,0:T(8,128)S(1)} %get-tuple-element.820), channel_id=1, source_target_pairs={{0,12},{1,13},{2,14},{3,15},{4,8},{5,9},{6,10},{7,11},{8,4},{9,5},... | collective-permute-start | bytes 196616 | tf_op jit(solution)/shard_map/ppermute | solution.py:292
  21.6 6.6 %collective-permute-start.221 = (f32[128,128]{1,0:T(8,128)S(1)}, f32[128,128]{1,0:T(8,128)S(1)}, u32[]{:S(2)}, u32[]{:S(2)}) collective-permute-start(f32[128,128]{1,0:T(8,128)S(1)} %get-tuple-element.820), channel_id=1, source_target_pairs={{0,8},{1,9},{2,10},{3,11},{4,12},{5,13},{6,14},{7,15},{8,0},{9,1},... | collective-permute-start | bytes 196616 | tf_op jit(solution)/shard_map/ppermute | solution.py:292
  22.1 6.1 %collective-permute-start.220 = (f32[128,128]{1,0:T(8,128)S(1)}, f32[128,128]{1,0:T(8,128)S(1)}, u32[]{:S(2)}, u32[]{:S(2)}) collective-permute-start(f32[128,128]{1,0:T(8,128)S(1)} %get-tuple-element.820), channel_id=1, source_target_pairs={{0,4},{1,5},{2,6},{3,7},{4,0},{5,1},{6,2},{7,3},{8,12},{9,13},{10,... | collective-permute-start | bytes 196616 | tf_op jit(solution)/shard_map/ppermute | solution.py:292
  22.6 5.6 %collective-permute-start.226 = (f32[128,128]{1,0:T(8,128)S(1)}, f32[128,128]{1,0:T(8,128)S(1)}, u32[]{:S(2)}, u32[]{:S(2)}) collective-permute-start(f32[128,128]{1,0:T(8,128)S(1)} %collective-permute-done.223), channel_id=1, source_target_pairs={{0,12},{1,13},{2,14},{3,15},{4,8},{5,9},{6,10},{7,11},{8,4},{9,5},... | collective-permute-start | bytes 196616 | tf_op jit(solution)/shard_map/ppermute | solution.py:292
  25.1 4.3 %collective-permute-start.225 = (f32[128,128]{1,0:T(8,128)S(1)}, f32[128,128]{1,0:T(8,128)S(1)}, u32[]{:S(2)}, u32[]{:S(2)}) collective-permute-start(f32[128,128]{1,0:T(8,128)S(1)} %collective-permute-done.223), channel_id=1, source_target_pairs={{0,8},{1,9},{2,10},{3,11},{4,12},{5,13},{6,14},{7,15},{8,0},{9,1},... | collective-permute-start | bytes 196616 | tf_op jit(solution)/shard_map/ppermute | solution.py:292
  25.6 4.3 %collective-permute-start.224 = (f32[128,128]{1,0:T(8,128)S(1)}, f32[128,128]{1,0:T(8,128)S(1)}, u32[]{:S(2)}, u32[]{:S(2)}) collective-permute-start(f32[128,128]{1,0:T(8,128)S(1)} %collective-permute-done.223), channel_id=1, source_target_pairs={{0,4},{1,5},{2,6},{3,7},{4,0},{5,1},{6,2},{7,3},{8,12},{9,13},{10,... | collective-permute-start | bytes 196616 | tf_op jit(solution)/shard_map/ppermute | solution.py:292
  33.2 7.2 %collective-permute-start.73 = (f32[128,128]{1,0:T(8,128)S(1)}, f32[128,128]{1,0:T(8,128)}, u32[]{:S(2)}, u32[]{:S(2)}) collective-permute-start(f32[128,128]{1,0:T(8,128)S(1)} %param.33), channel_id=1, source_target_pairs={{0,28},{1,29},{2,30},{3,31},{4,24},{5,25},{6,26},{7,27},{8,20},{9,... | collective-permute-start | bytes 196616 | tf_op jit(solution)/shard_map/cond/branch_17_fun/ppermute | solution.py:292
  36.7 5.3 %collective-permute-start.72 = (f32[128,128]{1,0:T(8,128)S(1)}, f32[128,128]{1,0:T(8,128)}, u32[]{:S(2)}, u32[]{:S(2)}) collective-permute-start(f32[128,128]{1,0:T(8,128)S(1)} %param.33), channel_id=1, source_target_pairs={{0,16},{1,17},{2,18},{3,19},{4,20},{5,21},{6,22},{7,23},{8,24},{9,... | collective-permute-start | bytes 196616 | tf_op jit(solution)/shard_map/cond/branch_17_fun/ppermute | solution.py:292
  44.2 0.6 %copy-start.2 = (f32[128,128]{1,0:T(8,128)}, f32[128,128]{1,0:T(8,128)S(1)}, u32[]{:S(2)}) copy-start(f32[128,128]{1,0:T(8,128)S(1)} %get-tuple-element.1382) | copy-start | bytes 196612
